TPU v7x, 32 devices: a whole 2x2x4 slice. The times are simulated.
32 devices in a mesh: groups: 2 (over x), shard: 8 (over z, core), cam: 2 (over y).
Axes of the slice: x: 2, y: 2, z: 4, core: 2. Of those that a mesh axis runs over, the one named last changes fastest.
Arguments:
- params: float32 [59, 65536], P(None, ('groups', 'shard')), parts along dimension 1, as said below
- cameras: float32 [4, 4], P('groups'), parts along dimension 0, may hold values from -0.02 to 0.02
- send_rows: int32 [4, 8, 2048], P(('groups', 'cam'), 'shard'), parts along dimension 0, may hold values from 0 to 4095
- tile_ids: int32 [4, 64], P(('groups', 'cam'), 'shard'), parts along dimension 0, may hold values from 0 to 63, as said below
- tile_counts: int32 [4, 64], P(('groups', 'cam'), 'shard'), parts along dimension 0, may hold values from 0 to 512, as said below
- tile_lists: int32 [4, 64, 512], P(('groups', 'cam'), 'shard'), parts along dimension 0, may hold values from 0 to 2047, as said below
- targets: float32 [4, 64, 3, 256], P(('groups', 'cam'), 'shard'), parts along dimension 0, may hold values from 0 to 1
Outputs:
- rendered: float32 [4, 64, 3, 256], P(('groups', 'cam'), 'shard'), parts along dimension 0
- param_grad: float32 [59, 65536], P(None, ('groups', 'shard', 'cam')), parts along dimension 1
There are 2 independent parts, one for each index of `groups`. A program takes and returns all parts, laid end to end along the dimension named above; each array names one. Nothing has to cross between parts.
Inputs may be any that keep to these rules, and one draw needn't show every extreme that they name: `params`: row 2 of every column (the centre's third coordinate) lies in 4 to 8, and row 6 (the quaternion's first entry) lies in 1 to 2. `tile_ids`: each view's row names every grid tile once. `tile_counts`: the 8 tiles of one renderer come in pairs whose counts sum to 512, one pair being 512 and 0 in every renderer, so a renderer's counts sum to 2048. `tile_lists`: entries before a tile's count name slots of its renderer that hold distinct Gaussians, in order of increasing depth (row 2 of params); over one renderer's tiles every one of its 2048 slots is named exactly once. Entries at or after the count are arbitrary slots.
All inputs are finite; a program needn't handle non-finite values.
Results may differ from a plain program's by a relative error of at most 0.0003.
Values sent between devices are 32-bit elements; how exact they have to be, the bound alone decides.
A program may use at most 128 MiB of HBM per device.

v0:
```python
import functools

import jax
import jax.numpy as jnp
import numpy as np
from jax import lax
from jax.experimental import pallas as pl
from jax.experimental.pallas import tpu as pltpu
from jax.sharding import PartitionSpec as P

PIX = 256
TILE_COLS = 8
LANES = 128
FEATS = 9
ROWS = 16
CLAMP = 0.99
FOCAL_LENGTH = 1000.0
SH_ZERO = 0.28209479177387814
SH_ONE = 0.4886025119029199
SH_TWO = (
    1.0925484305920792,
    -1.0925484305920792,
    0.31539156525252005,
    -1.0925484305920792,
    0.5462742152960396,
)
SH_THREE = (
    -0.5900435899266435,
    2.890611442640554,
    -0.4570457994644658,
    0.3731763325901154,
    -0.4570457994644658,
    1.445305721320277,
    -0.5900435899266435,
)
F32 = jnp.float32
BF16 = jnp.bfloat16
NT = (((1,), (1,)), ((), ()))
VMEM_LIMIT = 48 * 1024 * 1024


def unit_like(value):
    if isinstance(value, Pair):
        return Pair(jnp.ones_like(value.high), jnp.zeros_like(value.low))
    return jnp.ones_like(value)


def harmonics(dir_x, dir_y, dir_z):
    square_x = dir_x * dir_x
    square_y = dir_y * dir_y
    square_z = dir_z * dir_z
    return [
        unit_like(dir_x) * SH_ZERO,
        -SH_ONE * dir_y,
        SH_ONE * dir_z,
        -SH_ONE * dir_x,
        SH_TWO[0] * dir_x * dir_y,
        SH_TWO[1] * dir_y * dir_z,
        SH_TWO[2] * (2.0 * square_z - square_x - square_y),
        SH_TWO[3] * dir_x * dir_z,
        SH_TWO[4] * (square_x - square_y),
        SH_THREE[0] * dir_y * (3.0 * square_x - square_y),
        SH_THREE[1] * dir_x * dir_y * dir_z,
        SH_THREE[2] * dir_y * (4.0 * square_z - square_x - square_y),
        SH_THREE[3] * dir_z * (2.0 * square_z - 3.0 * square_x - 3.0 * square_y),
        SH_THREE[4] * dir_x * (4.0 * square_z - square_x - square_y),
        SH_THREE[5] * dir_z * (square_x - square_y),
        SH_THREE[6] * dir_x * (square_x - 3.0 * square_y),
    ]


def camera_of(cam_ref, view):
    angle = jnp.full((1, LANES), cam_ref[view, 0], F32)
    return (jnp.cos(angle), jnp.sin(angle), cam_ref[view, 1], cam_ref[view, 2], cam_ref[view, 3])


def geometry(camera, centre, source):
    cosine, sine, shift_x, shift_y, shift_z = camera
    world_x, world_y, world_z = source[0:3]
    view_x = cosine * world_x - sine * world_y + shift_x
    view_y = sine * world_x + cosine * world_y + shift_y
    inverse_z = 1.0 / (world_z + shift_z)
    mean_u = FOCAL_LENGTH * view_x * inverse_z + centre[0]
    mean_v = FOCAL_LENGTH * view_y * inverse_z + centre[1]
    scale_sq = [jnp.exp(2.0 * value) for value in source[3:6]]
    norm = lax.rsqrt(sum(value * value for value in source[6:10]))
    quat_w, quat_x, quat_y, quat_z = [value * norm for value in source[6:10]]
    rotation = [
        [
            1.0 - 2.0 * (quat_y * quat_y + quat_z * quat_z),
            2.0 * (quat_x * quat_y - quat_w * quat_z),
            2.0 * (quat_x * quat_z + quat_w * quat_y),
        ],
        [
            2.0 * (quat_x * quat_y + quat_w * quat_z),
            1.0 - 2.0 * (quat_x * quat_x + quat_z * quat_z),
            2.0 * (quat_y * quat_z - quat_w * quat_x),
        ],
        [
            2.0 * (quat_x * quat_z - quat_w * quat_y),
            2.0 * (quat_y * quat_z + quat_w * quat_x),
            1.0 - 2.0 * (quat_x * quat_x + quat_y * quat_y),
        ],
    ]
    focal_z = FOCAL_LENGTH * inverse_z
    first = [focal_z * cosine, -focal_z * sine, -focal_z * view_x * inverse_z]
    second = [focal_z * sine, focal_z * cosine, -focal_z * view_y * inverse_z]
    first_q = [sum(first[i] * rotation[i][k] for i in range(3)) for k in range(3)]
    second_q = [sum(second[i] * rotation[i][k] for i in range(3)) for k in range(3)]
    cov_a = sum(first_q[k] * first_q[k] * scale_sq[k] for k in range(3)) + 0.3
    cov_b = sum(first_q[k] * second_q[k] * scale_sq[k] for k in range(3))
    cov_c = sum(second_q[k] * second_q[k] * scale_sq[k] for k in range(3)) + 0.3
    inverse_det = 1.0 / (cov_a * cov_c - cov_b * cov_b)
    return [mean_u, mean_v, cov_c * inverse_det, -cov_b * inverse_det, cov_a * inverse_det]


def basis_of(camera, world):
    cosine, sine, shift_x, shift_y, shift_z = camera
    ray_x = world[0] + (cosine * shift_x + sine * shift_y)
    ray_y = world[1] + (-sine * shift_x + cosine * shift_y)
    ray_z = world[2] + shift_z
    inverse = lax.rsqrt(ray_x * ray_x + ray_y * ray_y + ray_z * ray_z)
    return harmonics(ray_x * inverse, ray_y * inverse, ray_z * inverse)


def two_sum(a, b):
    total = a + b
    part = total - a
    return total, (a - (total - part)) + (b - part)


def two_prod(a, b):
    total = a * b
    wide_a, wide_b = 4097.0 * a, 4097.0 * b
    a_high = wide_a - (wide_a - a)
    b_high = wide_b - (wide_b - b)
    a_low, b_low = a - a_high, b - b_high
    error = ((a_high * b_high - total) + a_high * b_low + a_low * b_high) + a_low * b_low
    return total, error


class Pair:
    def __init__(self, high, low):
        self.high, self.low = high, low

    def __add__(self, other):
        if not isinstance(other, Pair):
            other = Pair(other, 0.0)
        total, error = two_sum(self.high, other.high)
        return Pair(*two_sum(total, error + (self.low + other.low)))

    __radd__ = __add__

    def __neg__(self):
        return Pair(-self.high, -self.low)

    def __sub__(self, other):
        return self + (-other)

    def __mul__(self, other):
        if not isinstance(other, Pair):
            if isinstance(other, float):
                high = float(np.float32(other))
                other = Pair(jnp.full_like(self.high, high), other - high)
            else:
                other = Pair(other, 0.0)
        total, error = two_prod(self.high, other.high)
        return Pair(*two_sum(total, error + (self.high * other.low + self.low * other.high)))

    __rmul__ = __mul__


def colour_totals(camera, world, par_ref):
    cosine, sine, shift_x, shift_y, shift_z = camera
    plain = basis_of(camera, world)
    zero = jnp.zeros_like(world[0])
    first = cosine * shift_x + sine * shift_y
    second = -sine * shift_x + cosine * shift_y
    ray = [Pair(*two_sum(world[0], zero + first)), Pair(*two_sum(world[1], zero + second))]
    ray.append(Pair(*two_sum(world[2], zero + shift_z)))
    square = ray[0] * ray[0] + ray[1] * ray[1] + ray[2] * ray[2]
    guess = lax.rsqrt(square.high)
    rest = (square * guess) * guess + (zero - 1.0)
    inverse = Pair(*two_sum(guess, -0.5 * guess * (rest.high + rest.low)))
    direction = [value * inverse for value in ray]
    basis = harmonics(*direction)
    totals = []
    for channel in range(3):
        coeffs = [par_ref[11 + 16 * channel + k] for k in range(16)]
        total = Pair(zero + 0.5, zero)
        for k in range(16):
            total = total + basis[k] * coeffs[k]
        careful = total.high + total.low
        simple = 0.5 + sum(plain[k] * coeffs[k] for k in range(16))
        totals.append(jnp.where(careful - careful == 0.0, careful, simple))
    return totals


def pieces_of(value, count):
    parts = []
    for _ in range(count - 1):
        part = value.astype(BF16).astype(F32)
        parts.append(part)
        value = value - part
    parts.append(value)
    return parts


def split_pair(value):
    high = value.astype(BF16)
    return high, (value - high.astype(F32)).astype(BF16)


def one_hot(rows, index):
    grid = lax.broadcasted_iota(jnp.int32, (rows, index.shape[1]), 0)
    return grid == index


def as_bf16(mask):
    return jnp.where(mask, 1.0, 0.0).astype(BF16)


def peers_of(axis, count):
    me = lax.axis_index(axis)
    return me, [lax.rem(me + step, count) for step in range(1, count)]


def greet(groups):
    barrier = pltpu.get_barrier_semaphore()
    for axis, partners in groups:
        for partner in partners:
            pl.semaphore_signal(
                barrier, inc=1, device_id={axis: partner}, device_id_type=pl.DeviceIdType.MESH
            )
    pl.semaphore_wait(barrier, sum(len(partners) for _, partners in groups))


def push(axis, partner, source, target, send_sem, recv_sem):
    return pltpu.make_async_remote_copy(
        src_ref=source,
        dst_ref=target,
        send_sem=send_sem,
        recv_sem=recv_sem,
        device_id={axis: partner},
        device_id_type=pl.DeviceIdType.MESH,
    )


def project_kernel(centre, cam_ref, par_ref, table_ref, gate_ref):
    camera = camera_of(cam_ref, lax.axis_index("cam"))
    groups = par_ref.shape[1]
    source = [par_ref[k] for k in range(10)]
    feats = geometry(camera, centre, source)
    feats.append(1.0 / (1.0 + jnp.exp(-par_ref[10])))
    for channel, total in enumerate(colour_totals(camera, source[0:3], par_ref)):
        feats.append(jnp.maximum(0.0, total))
        gate_ref[channel] = jnp.where(total > 0.0, 1.0, jnp.where(total == 0.0, 0.5, 0.0))
    for f in range(FEATS):
        for piece, value in enumerate(pieces_of(feats[f], 3)):
            table_ref[pl.ds((f * 3 + piece) * groups, groups), :] = value.astype(BF16)


def send_kernel(shards, table, rows_ref, out_ref, staged, landed, send_sem, recv_sem):
    me, partners = peers_of("shard", shards)
    greet([("shard", partners)])
    groups = table.shape[0] // (3 * FEATS)
    cap = out_ref.shape[2]

    def gathered(r):
        index = rows_ref[pl.ds(r, 1), :]
        low = as_bf16(one_hot(LANES, index & (LANES - 1)))
        high = one_hot(groups, lax.shift_right_logical(index, 7))
        found = jnp.dot(table[...], low, preferred_element_type=F32)
        values = []
        for f in range(FEATS):
            base = f * 3 * groups
            value = (
                found[base : base + groups]
                + found[base + groups : base + 2 * groups]
                + found[base + 2 * groups : base + 3 * groups]
            )
            values.append(jnp.sum(jnp.where(high, value, 0.0), axis=0, keepdims=True))
        return stack_rows(values, ROWS)

    copies = []
    for step, partner in enumerate(partners):
        staged[step] = gathered(partner)
        copy = push(
            "shard",
            partner,
            staged.at[step],
            landed.at[step],
            send_sem.at[step],
            recv_sem.at[step],
        )
        copy.start()
        copies.append(copy)
    out_ref[me] = gathered(me)
    for step, copy in enumerate(copies):
        copy.wait_recv()
        out_ref[lax.rem(me + (shards - 1 - step), shards)] = landed[step]
    for copy in copies:
        copy.wait_send()


def stack_rows(values, rows):
    row = lax.broadcasted_iota(jnp.int32, (rows, values[0].shape[1]), 0)
    out = jnp.zeros(row.shape, F32)
    for k, value in enumerate(values):
        out = jnp.where(row == k, value, out)
    return out


def mono_value(kind, x, y):
    return jnp.where(
        kind == 0,
        1.0,
        jnp.where(
            kind == 1,
            x,
            jnp.where(
                kind == 2,
                y,
                jnp.where(
                    kind == 3,
                    x * x,
                    jnp.where(kind == 4, x * y, jnp.where(kind == 5, y * y, 0.0)),
                ),
            ),
        ),
    )


def pixel_offset(index):
    return (index & 15).astype(F32) - 7.5, lax.shift_right_logical(index, 4).astype(F32) - 7.5


def render_kernel(
    tiles,
    blocks,
    ids_ref,
    counts_ref,
    feats_ref,
    lists_ref,
    wanted_ref,
    image_ref,
    grad_ref,
    table,
    mono_row,
    upper,
    lower,
    keep_x,
    keep_wh,
    keep_wl,
    keep_f,
    carry,
    image,
    acc,
):
    shards, _, cap = feats_ref.shape
    per = cap // LANES
    groups = shards * per
    for h in range(groups):
        s, part = h // per, h % per
        block = feats_ref[s, :, part * LANES : (part + 1) * LANES]
        table[pl.ds(h * 48, 48), :] = jnp.concatenate(pieces_of(block, 3), axis=0).astype(BF16)
    k = lax.broadcasted_iota(jnp.int32, (ROWS, PIX), 0)
    x, y = pixel_offset(lax.broadcasted_iota(jnp.int32, (ROWS, PIX), 1))
    mono_row[...] = mono_value(k, x, y).astype(BF16)
    n = lax.broadcasted_iota(jnp.int32, (LANES, 2 * LANES), 0)
    m = lax.broadcasted_iota(jnp.int32, (LANES, 2 * LANES), 1)
    upper[...] = as_bf16((n < m) | (m >= LANES))
    lower[...] = as_bf16((n > m) | (m >= LANES))
    acc[...] = jnp.zeros_like(acc)
    lane = lax.broadcasted_iota(jnp.int32, (1, LANES), 1)

    def one_tile(t, _):
        count = counts_ref[0, t]
        grid_id = ids_ref[0, t]
        origin_x = (16 * lax.rem(grid_id, TILE_COLS) + 8).astype(F32)
        origin_y = (16 * lax.div(grid_id, TILE_COLS) + 8).astype(F32)
        steps = lax.div(count + (LANES - 1), LANES)
        carry[...] = jnp.zeros_like(carry)
        image[...] = jnp.zeros_like(image)

        def entry_index(j):
            return lists_ref[pl.ds(t * blocks + j, 1), :]

        def forward(j, _):
            index = entry_index(j)
            low = as_bf16(one_hot(LANES, index & (LANES - 1)))
            high = lax.shift_right_logical(index, 7)
            found = jnp.dot(table[...], low, preferred_element_type=F32)
            total = jnp.zeros((48, LANES), F32)
            for h in range(groups):
                total = total + jnp.where(high == h, found[h * 48 : (h + 1) * 48], 0.0)
            feats = total[0:16] + total[16:32] + total[32:48]
            keep_f[j] = feats
            ux = feats[0:1] - origin_x
            uy = feats[1:2] - origin_y
            c0, c1, c2 = feats[2:3], feats[3:4], feats[4:5]
            valid = j * LANES + lane < count
            offset = lax.broadcasted_iota(jnp.int32, (16, LANES), 0).astype(F32) - 7.5
            dx = offset - ux
            dy = offset - uy
            along_x = jnp.where(valid, -0.5 * c0 * dx * dx, 0.0)
            cross = jnp.where(valid, -c1 * dx, 0.0)
            along_y = jnp.where(valid, -0.5 * c2 * dy * dy, -1e30)
            value = feats[5:6] * jnp.exp(
                jnp.concatenate(
                    [
                        (along_x + along_y[r : r + 1]) + cross * dy[r : r + 1]
                        for r in range(PIX // 16)
                    ],
                    axis=0,
                )
            )
            keep_x[j] = value
            alpha = jnp.minimum(CLAMP, value)
            log_high, log_low = split_pair(jnp.log(1.0 - alpha))
            before = jnp.dot(log_high, upper[...], preferred_element_type=F32) + jnp.dot(
                log_low, upper[...], preferred_element_type=F32
            )
            held = carry[...]
            weight = alpha * jnp.exp(before[:, :LANES] + held)
            carry[...] = held + before[:, LANES:]
            w_high, w_low = split_pair(weight)
            keep_wh[j] = w_high
            keep_wl[j] = w_low
            colour = stack_rows([feats[6:7], feats[7:8], feats[8:9]], 8)
            colour = jnp.concatenate(pieces_of(colour, 2), axis=0).astype(BF16)
            drawn = lax.dot_general(colour, w_high, NT, preferred_element_type=F32)
            drawn = drawn + lax.dot_general(colour, w_low, NT, preferred_element_type=F32)
            image[...] += drawn[0:8] + drawn[8:16]
            return 0

        lax.fori_loop(0, steps, forward, 0)
        shown = image[0:3]
        image_ref[t] = shown
        slope = (shown - wanted_ref[t]) * (1.0 / PIX)
        slope = stack_rows([slope[0:1], slope[1:2], slope[2:3]], 8)
        g_high, g_low = pieces_of(slope, 2)
        g_row = jnp.concatenate([g_high, g_low], axis=0).astype(BF16)
        g_col = jnp.transpose(jnp.concatenate([g_high, g_high, g_low, g_low], axis=0)).astype(BF16)
        carry[...] = jnp.zeros_like(carry)

        def backward(step, _):
            j = steps - 1 - step
            feats = keep_f[j]
            colour = stack_rows([feats[6:7], feats[7:8], feats[8:9]], 8)
            c_high, c_low = pieces_of(colour, 2)
            colour = jnp.concatenate([c_high, c_low, c_high, c_low], axis=0).astype(BF16)
            pull = jnp.dot(g_col, colour, preferred_element_type=F32)
            w_high, w_low = keep_wh[j], keep_wl[j]
            share = (w_high.astype(F32) + w_low.astype(F32)) * pull
            s_high, s_low = split_pair(share)
            after = jnp.dot(s_high, lower[...], preferred_element_type=F32) + jnp.dot(
                s_low, lower[...], preferred_element_type=F32
            )
            held = carry[...]
            behind = after[:, :LANES] + held
            carry[...] = held + after[:, LANES:]
            value = keep_x[j]
            free = value < CLAMP
            odds = value / (1.0 - jnp.minimum(value, CLAMP))
            p_high, p_low = split_pair(jnp.where(free, share - odds * behind, 0.0))
            mom = jnp.dot(mono_row[...], p_high, preferred_element_type=F32) + jnp.dot(
                mono_row[...], p_low, preferred_element_type=F32
            )
            tint = jnp.dot(g_row, w_high, preferred_element_type=F32) + jnp.dot(
                g_row, w_low, preferred_element_type=F32
            )
            tint = tint[0:8] + tint[8:16]
            ux = feats[0:1] - origin_x
            uy = feats[1:2] - origin_y
            c0, c1, c2 = feats[2:3], feats[3:4], feats[4:5]
            m0, mx, my = mom[0:1], mom[1:2], mom[2:3]
            px = mx - ux * m0
            py = my - uy * m0
            pxx = mom[3:4] - ux * (mx + px)
            pxy = mom[4:5] - ux * my - uy * px
            pyy = mom[5:6] - uy * (my + py)
            grads = stack_rows(
                [
                    c0 * px + c1 * py,
                    c2 * py + c1 * px,
                    -0.5 * pxx,
                    -pxy,
                    -0.5 * pyy,
                    m0,
                    tint[0:1],
                    tint[1:2],
                    tint[2:3],
                ],
                ROWS,
            )
            grads = jnp.concatenate(pieces_of(grads, 2), axis=0)
            index = entry_index(j)
            low = as_bf16(one_hot(LANES, index & (LANES - 1)))
            high = lax.shift_right_logical(index, 7)
            valid = j * LANES + lane < count
            grads = jnp.where(valid, grads, 0.0)
            spread = jnp.concatenate(
                [jnp.where(high == h, grads, 0.0) for h in range(groups)], axis=0
            ).astype(BF16)
            acc[...] += lax.dot_general(spread, low, NT, preferred_element_type=F32)
            return 0

        lax.fori_loop(0, steps, backward, 0)
        return 0

    lax.fori_loop(0, tiles, one_tile, 0)
    for h in range(groups):
        s, part = h // per, h % per
        grad_ref[s, :, part * LANES : (part + 1) * LANES] = (
            acc[pl.ds(h * 32, 16), :] + acc[pl.ds(h * 32 + 16, 16), :]
        )


def return_kernel(
    shards,
    cams,
    centre,
    cam_ref,
    par_ref,
    slot_ref,
    rows_ref,
    gate_ref,
    out_ref,
    acc,
    landed,
    mine,
    other,
    shard_send,
    shard_recv,
    cam_send,
    cam_recv,
):
    me, partners = peers_of("shard", shards)
    here, views = peers_of("cam", cams)
    greet([("shard", partners), ("cam", views)])
    size = out_ref.shape[1]
    groups = cams * size
    copies = []
    for step, partner in enumerate(partners):
        copy = push(
            "shard",
            partner,
            slot_ref.at[partner],
            landed.at[step],
            shard_send.at[step],
            shard_recv.at[step],
        )
        copy.start()
        copies.append(copy)

    def scattered(r, value):
        index = rows_ref[pl.ds(r, 1), :]
        low = as_bf16(one_hot(LANES, index & (LANES - 1)))
        high = one_hot(groups, lax.shift_right_logical(index, 7))
        parts = pieces_of(value, 2)
        spread = jnp.concatenate(
            [
                jnp.where(high, part[f : f + 1], 0.0).astype(BF16)
                for f in range(FEATS)
                for part in parts
            ],
            axis=0,
        )
        return lax.dot_general(spread, low, NT, preferred_element_type=F32)

    acc[...] = scattered(me, slot_ref[me])
    for step, copy in enumerate(copies):
        copy.wait_recv()
        acc[...] += scattered(lax.rem(me + (shards - 1 - step), shards), landed[step])
    for f in range(FEATS):
        value = acc[pl.ds(2 * f * groups, groups), :] + acc[pl.ds((2 * f + 1) * groups, groups), :]
        if f >= 6:
            value = value * gate_ref[f - 6]
        for c in range(cams):
            mine[c, f] = value[c * size : (c + 1) * size]
    swaps = []
    for step, view in enumerate(views):
        copy = push(
            "cam", view, mine.at[view], other.at[step], cam_send.at[step], cam_recv.at[step]
        )
        copy.start()
        swaps.append(copy)
    source = [par_ref[k] for k in range(10)]
    keep = 1.0 / (1.0 + jnp.exp(par_ref[10]))

    def one_view(view, feature_grad, first):
        camera = camera_of(cam_ref, view)
        _, pull_geometry = jax.vjp(lambda *s: geometry(camera, centre, s), *source)
        head = list(pull_geometry([feature_grad(f) for f in range(5)]))
        basis, pull_basis = jax.vjp(lambda *w: basis_of(camera, w), *source[0:3])
        tints = [feature_grad(6 + channel) for channel in range(3)]
        cotangent = [
            sum(tints[channel] * par_ref[11 + 16 * channel + k] for channel in range(3))
            for k in range(16)
        ]
        for k, value in enumerate(pull_basis(cotangent)):
            head[k] = head[k] + value

        def put(k, value):
            if first:
                out_ref[k] = value
            else:
                out_ref[k] += value

        for k in range(10):
            put(k, head[k])
        put(10, keep * feature_grad(5))
        for channel in range(3):
            for k in range(16):
                put(11 + 16 * channel + k, tints[channel] * basis[k])

    one_view(here, lambda f: mine[here, f], True)
    for step, copy in enumerate(swaps):
        copy.wait_recv()
        one_view(
            lax.rem(here + (cams - 1 - step), cams), lambda f, step=step: other[step, f], False
        )
    for copy in copies + swaps:
        copy.wait_send()


def local_params():
    return pltpu.CompilerParams(vmem_limit_bytes=VMEM_LIMIT)


def remote_params(number):
    return pltpu.CompilerParams(
        vmem_limit_bytes=VMEM_LIMIT, collective_id=number, has_side_effects=True
    )


VM = pl.BlockSpec(memory_space=pltpu.VMEM)
SM = pl.BlockSpec(memory_space=pltpu.SMEM)


def per_device(params, cameras, send_rows, tile_ids, tile_counts, tile_lists, targets):
    shards = lax.axis_size("shard")
    cams = lax.axis_size("cam")
    tiles, length = tile_lists.shape[1:]
    blocks = length // LANES
    centre = (8.0 * TILE_COLS, 8.0 * (shards * tiles // TILE_COLS))
    slots = send_rows.shape[2]
    cap = slots // shards
    groups = params.shape[1] // LANES
    size = groups // cams
    wide = params.reshape(params.shape[0], groups, LANES)
    rows = send_rows.reshape(shards, cap)
    table, gates = pl.pallas_call(
        functools.partial(project_kernel, centre),
        out_shape=(
            jax.ShapeDtypeStruct((3 * FEATS * groups, LANES), BF16),
            jax.ShapeDtypeStruct((3, groups, LANES), F32),
        ),
        in_specs=[SM, VM],
        out_specs=(VM, VM),
        compiler_params=local_params(),
        name="project",
    )(cameras, wide)
    links = pltpu.SemaphoreType.DMA((shards - 1,))
    arrived = pl.pallas_call(
        functools.partial(send_kernel, shards),
        out_shape=jax.ShapeDtypeStruct((shards, ROWS, cap), F32),
        in_specs=[VM, VM],
        out_specs=VM,
        scratch_shapes=[
            pltpu.VMEM((shards - 1, ROWS, cap), F32),
            pltpu.VMEM((shards - 1, ROWS, cap), F32),
            links,
            links,
        ],
        compiler_params=remote_params(0),
        name="send",
    )(table, rows)
    image, slot_grad = pl.pallas_call(
        functools.partial(render_kernel, tiles, blocks),
        out_shape=(
            jax.ShapeDtypeStruct((tiles, 3, PIX), F32),
            jax.ShapeDtypeStruct((shards, ROWS, cap), F32),
        ),
        in_specs=[SM, SM, VM, VM, VM],
        out_specs=(VM, VM),
        scratch_shapes=[
            pltpu.VMEM((slots // LANES * 48, LANES), BF16),
            pltpu.VMEM((ROWS, PIX), BF16),
            pltpu.VMEM((LANES, 2 * LANES), BF16),
            pltpu.VMEM((LANES, 2 * LANES), BF16),
            pltpu.VMEM((blocks, PIX, LANES), F32),
            pltpu.VMEM((blocks, PIX, LANES), BF16),
            pltpu.VMEM((blocks, PIX, LANES), BF16),
            pltpu.VMEM((blocks, ROWS, LANES), F32),
            pltpu.VMEM((PIX, LANES), F32),
            pltpu.VMEM((8, PIX), F32),
            pltpu.VMEM((slots // LANES * 32, LANES), F32),
        ],
        compiler_params=local_params(),
        name="render",
    )(
        tile_ids,
        tile_counts,
        arrived,
        tile_lists[0].reshape(tiles * blocks, LANES),
        targets[0],
    )
    mine = lax.dynamic_slice_in_dim(wide, lax.axis_index("cam") * size, size, axis=1)
    grad = pl.pallas_call(
        functools.partial(return_kernel, shards, cams, centre),
        out_shape=jax.ShapeDtypeStruct((params.shape[0], size, LANES), F32),
        in_specs=[SM, VM, VM, VM, VM],
        out_specs=VM,
        scratch_shapes=[
            pltpu.VMEM((2 * FEATS * groups, LANES), F32),
            pltpu.VMEM((shards - 1, ROWS, cap), F32),
            pltpu.VMEM((cams, FEATS, size, LANES), F32),
            pltpu.VMEM((cams - 1, FEATS, size, LANES), F32),
            links,
            links,
            pltpu.SemaphoreType.DMA((cams - 1,)),
            pltpu.SemaphoreType.DMA((cams - 1,)),
        ],
        compiler_params=remote_params(1),
        name="return_pull",
    )(cameras, mine, slot_grad, rows, gates)
    return (image[None], grad.reshape(params.shape[0], size * LANES))


def solution(mesh):
    placed = (
        P(None, ("groups", "shard")),
        P("groups", None),
        P(("groups", "cam"), "shard", None),
        P(("groups", "cam"), "shard"),
        P(("groups", "cam"), "shard"),
        P(("groups", "cam"), "shard", None),
        P(("groups", "cam"), "shard", None, None),
    )
    return jax.shard_map(
        per_device,
        mesh=mesh,
        in_specs=placed,
        out_specs=(P(("groups", "cam"), "shard", None, None), P(None, ("groups", "shard", "cam"))),
        check_vma=False,
    )
```

profile of v0, /device:TPU:0, one launch (start us, length us, event | category | flops | bytes accessed | tf_op | source)
XLA Modules:
  0.0 61.2 jit_solution(15584449166006375977)
XLA Ops:
  0.6 1.4 %copy.11 = f32[8,8,32,128]{3,2,1,0:T(8,128)S(1)} copy(f32[8,8,32,128]{3,1,2,0:T(8,128)} %bitcast.14) | data formatting | bytes 2097152
  2.0 0.0 copy-start
  2.1 0.1 slice.par_ref
  2.1 0.6 copy-done
  2.7 0.0 copy-start.5
  2.7 2.4 %project.1 = (bf16[864,128]{1,0:T(8,128)(2,1)S(1)}, f32[3,32,128]{2,1,0:T(8,128)S(1)}) custom-call(f32[2,4]{1,0:T(2,128)S(1)} %copy-done, f32[59,32,128]{2,1,0:T(8,128)S(1)} %slice.par_ref), custom_call_target="tpu_custom_call" | custom-call | tf_op jit(solution)/shard_map/project/pallas_call | solution.py:654
  5.2 0.5 broadcast.3
  5.7 0.0 copy-done.5
  5.7 0.7 %reduce.3 = s32[2048]{0:T(1024)S(1)} reduce(s32[1,1,2048]{2,1,0:T(1,128)S(1)} %copy-done.5, s32[]{:T(128)} %broadcast.3), dimensions={0,1}, to_apply=%param.9.reduce_sub_computation.3 | reduce | bytes 16388 | tf_op args[2]
  6.4 0.0 copy-start.4
  6.4 10.0 %send.1.feats_ref = f32[8,16,256]{2,1,0:T(8,128)S(1)} custom-call(bf16[864,128]{1,0:T(8,128)(2,1)S(1)} %get-tuple-element.6.table, s32[8,256]{1,0:T(8,128)S(1)} %reshape.14.rows_ref), custom_call_target="tpu_custom_call" | custom-call | tf_op jit(solution)/shard_map/send/pallas_call | solution.py:666
  16.4 0.0 copy-done.4
  16.4 0.0 copy-start.3
  16.4 0.7 %copy-done.3 = f32[1,8,3,256]{3,1,2,0:T(8,128)S(1)} copy-done((f32[1,8,3,256]{3,1,2,0:T(8,128)S(1)}, f32[1,8,3,256]{3,1,2,0:T(8,128)}, u32[]{:S(2)}) %copy-start.3) | copy-done | bytes 24600
  17.2 0.0 copy-start.1
  17.2 0.0 copy-start.2
  17.2 0.6 %copy-done.1 = s32[1,8]{1,0:T(1,128)S(1)} copy-done((s32[1,8]{1,0:T(1,128)S(1)}, s32[1,8]{1,0:T(1,128)}, u32[]{:S(2)}) %copy-start.1) | copy-done | bytes 56
  17.8 0.0 copy-done.2
  17.8 29.0 %render.1 = (f32[8,3,256]{2,1,0:T(4,128)S(1)}, f32[8,16,256]{2,1,0:T(8,128)S(1)}) custom-call(s32[1,8]{1,0:T(1,128)S(1)} %copy-done.1, s32[1,8]{1,0:T(1,128)S(1)} %copy-done.2, f32[8,16,256]{2,1,0:T(8,128)S(1)} %send.1.feats_ref, s32[32,128]{1,0:T(8,128)S(1)} %reshape_squeeze.3.lists_ref, f32[8,3,256]{2,1,0:T(4,128)S(1)} %bitcast.10), custom_call_target="tpu_custom_call" | custom-call | tf_op jit(solution)/shard_map/render/pallas_call | solution.py:680
  46.9 0.6 %copy.10 = f32[1,8,3,256]{3,1,2,0:T(8,128)} copy(f32[1,8,3,256]{3,2,1,0:T(4,128)S(1)} %bitcast.11) | data formatting | bytes 49152
  47.5 12.7 %return_pull.1 = f32[59,16,128]{2,1,0:T(8,128)S(1)} custom-call(f32[2,4]{1,0:T(2,128)S(1)} %copy-done, f32[59,16,128]{2,1,0:T(8,128)S(1)} %constant_dynamic-slice_fusion.par_ref, f32[8,16,256]{2,1,0:T(8,128)S(1)} %get-tuple-element.8.slot_ref, s32[8,256]{1,0:T(8,128)S(1)} %reshape.14.rows_ref, f32[3,32,128]{2,1,0:T(8,128)S(1)} %get-tuple-element.9.gate_ref), custom_call_target="tpu_custom_call" | custom-call | tf_op jit(solution)/shard_map/return_pull/pallas_call | solution.py:711
  60.3 1.0 %copy.12 = f32[8,8,16,128]{3,1,2,0:T(8,128)} copy(f32[8,8,16,128]{3,2,1,0:T(8,128)S(1)} %bitcast.13) | data formatting | bytes 1048576
  (5 shorter events, 0.1 us)
Async XLA Ops:
  2.0 0.7 %copy-start = (f32[2,4]{1,0:T(2,128)S(1)}, f32[2,4]{1,0:T(2,128)}, u32[]{:S(2)}) copy-start(f32[2,4]{1,0:T(2,128)} %cam_ref.3) | copy-start | bytes 100
  2.7 3.0 %copy-start.5 = (s32[1,1,2048]{2,1,0:T(1,128)S(1)}, s32[1,1,2048]{2,1,0:T(1,128)}, u32[]{:S(2)}) copy-start(s32[1,1,2048]{2,1,0:T(1,128)} %param.9) | copy-start | bytes 24580
  6.4 10.0 %copy-start.4 = (s32[1,8,512]{2,1,0:T(8,128)S(1)}, s32[1,8,512]{2,1,0:T(8,128)}, u32[]{:S(2)}) copy-start(s32[1,8,512]{2,1,0:T(8,128)} %param.12) | copy-start | bytes 49156
  16.4 0.7 %copy-start.3 = (f32[1,8,3,256]{3,1,2,0:T(8,128)S(1)}, f32[1,8,3,256]{3,1,2,0:T(8,128)}, u32[]{:S(2)}) copy-start(f32[1,8,3,256]{3,1,2,0:T(8,128)} %param.13) | copy-start | bytes 73732
  17.2 0.7 %copy-start.1 = (s32[1,8]{1,0:T(1,128)S(1)}, s32[1,8]{1,0:T(1,128)}, u32[]{:S(2)}) copy-start(s32[1,8]{1,0:T(1,128)} %ids_ref.1) | copy-start | bytes 100
  17.2 0.7 %copy-start.2 = (s32[1,8]{1,0:T(1,128)S(1)}, s32[1,8]{1,0:T(1,128)}, u32[]{:S(2)}) copy-start(s32[1,8]{1,0:T(1,128)} %counts_ref.1) | copy-start | bytes 100
where the time goes:
time: 61.5 us; the launch traced here: 61.2 us
  Pallas kernels  54.2 us (88%)
  local copies, waits for them, and re-layouts  5.64 us (9%)
  between operations  0.76 us (1%)
  other arithmetic  0.67 us (1%)
    pallas_call x1, Pallas kernels, per_device(): pl.pallas_call(functools.partial(render_kernel, tiles, blocks), out_shape...  29 us
    pallas_call x1, Pallas kernels, per_device(): pl.pallas_call(functools.partial(return_kernel, shards, cams, centre), ou...  12.7 us
    pallas_call x1, Pallas kernels, per_device(): pl.pallas_call(functools.partial(send_kernel, shards), out_shape=jax.Shap...  10 us
    unnamed x18, local copies, waits for them, and re-layouts  5.54 us
    pallas_call x1, Pallas kernels, per_device(): pl.pallas_call(functools.partial(project_kernel, centre), out_shape=(jax....  2.43 us

commit v1 on v0

--- a/solution.py
+++ b/solution.py
@@ -11,6 +11,7 @@
 PIX = 256
 TILE_COLS = 8
 LANES = 128
+BLOCK = 256
 FEATS = 9
 ROWS = 16
 CLAMP = 0.99
@@ -335,6 +336,10 @@
     return (index & 15).astype(F32) - 7.5, lax.shift_right_logical(index, 4).astype(F32) - 7.5
 
 
+def widen(value):
+    return jnp.concatenate([value] * (BLOCK // LANES), axis=1)
+
+
 def render_kernel(
     tiles,
     blocks,
@@ -367,19 +372,19 @@
     k = lax.broadcasted_iota(jnp.int32, (ROWS, PIX), 0)
     x, y = pixel_offset(lax.broadcasted_iota(jnp.int32, (ROWS, PIX), 1))
     mono_row[...] = mono_value(k, x, y).astype(BF16)
-    n = lax.broadcasted_iota(jnp.int32, (LANES, 2 * LANES), 0)
-    m = lax.broadcasted_iota(jnp.int32, (LANES, 2 * LANES), 1)
-    upper[...] = as_bf16((n < m) | (m >= LANES))
-    lower[...] = as_bf16((n > m) | (m >= LANES))
+    n = lax.broadcasted_iota(jnp.int32, (BLOCK, BLOCK + LANES), 0)
+    m = lax.broadcasted_iota(jnp.int32, (BLOCK, BLOCK + LANES), 1)
+    upper[...] = as_bf16((n < m) | (m >= BLOCK))
+    lower[...] = as_bf16((n > m) | (m >= BLOCK))
     acc[...] = jnp.zeros_like(acc)
-    lane = lax.broadcasted_iota(jnp.int32, (1, LANES), 1)
+    lane = lax.broadcasted_iota(jnp.int32, (1, BLOCK), 1)
 
     def one_tile(t, _):
         count = counts_ref[0, t]
         grid_id = ids_ref[0, t]
         origin_x = (16 * lax.rem(grid_id, TILE_COLS) + 8).astype(F32)
         origin_y = (16 * lax.div(grid_id, TILE_COLS) + 8).astype(F32)
-        steps = lax.div(count + (LANES - 1), LANES)
+        steps = lax.div(count + (BLOCK - 1), BLOCK)
         carry[...] = jnp.zeros_like(carry)
         image[...] = jnp.zeros_like(image)
 
@@ -391,7 +396,7 @@
             low = as_bf16(one_hot(LANES, index & (LANES - 1)))
             high = lax.shift_right_logical(index, 7)
             found = jnp.dot(table[...], low, preferred_element_type=F32)
-            total = jnp.zeros((48, LANES), F32)
+            total = jnp.zeros((48, BLOCK), F32)
             for h in range(groups):
                 total = total + jnp.where(high == h, found[h * 48 : (h + 1) * 48], 0.0)
             feats = total[0:16] + total[16:32] + total[32:48]
@@ -399,8 +404,8 @@
             ux = feats[0:1] - origin_x
             uy = feats[1:2] - origin_y
             c0, c1, c2 = feats[2:3], feats[3:4], feats[4:5]
-            valid = j * LANES + lane < count
-            offset = lax.broadcasted_iota(jnp.int32, (16, LANES), 0).astype(F32) - 7.5
+            valid = j * BLOCK + lane < count
+            offset = lax.broadcasted_iota(jnp.int32, (16, BLOCK), 0).astype(F32) - 7.5
             dx = offset - ux
             dy = offset - uy
             along_x = jnp.where(valid, -0.5 * c0 * dx * dx, 0.0)
@@ -422,8 +427,8 @@
                 log_low, upper[...], preferred_element_type=F32
             )
             held = carry[...]
-            weight = alpha * jnp.exp(before[:, :LANES] + held)
-            carry[...] = held + before[:, LANES:]
+            weight = alpha * jnp.exp(before[:, :BLOCK] + widen(held))
+            carry[...] = held + before[:, BLOCK:]
             w_high, w_low = split_pair(weight)
             keep_wh[j] = w_high
             keep_wl[j] = w_low
@@ -458,8 +463,8 @@
                 s_low, lower[...], preferred_element_type=F32
             )
             held = carry[...]
-            behind = after[:, :LANES] + held
-            carry[...] = held + after[:, LANES:]
+            behind = after[:, :BLOCK] + widen(held)
+            carry[...] = held + after[:, BLOCK:]
             value = keep_x[j]
             free = value < CLAMP
             odds = value / (1.0 - jnp.minimum(value, CLAMP))
@@ -498,7 +503,7 @@
             index = entry_index(j)
             low = as_bf16(one_hot(LANES, index & (LANES - 1)))
             high = lax.shift_right_logical(index, 7)
-            valid = j * LANES + lane < count
+            valid = j * BLOCK + lane < count
             grads = jnp.where(valid, grads, 0.0)
             spread = jnp.concatenate(
                 [jnp.where(high == h, grads, 0.0) for h in range(groups)], axis=0
@@ -643,7 +648,7 @@
     shards = lax.axis_size("shard")
     cams = lax.axis_size("cam")
     tiles, length = tile_lists.shape[1:]
-    blocks = length // LANES
+    blocks = length // BLOCK
     centre = (8.0 * TILE_COLS, 8.0 * (shards * tiles // TILE_COLS))
     slots = send_rows.shape[2]
     cap = slots // shards
@@ -688,12 +693,12 @@
         scratch_shapes=[
             pltpu.VMEM((slots // LANES * 48, LANES), BF16),
             pltpu.VMEM((ROWS, PIX), BF16),
-            pltpu.VMEM((LANES, 2 * LANES), BF16),
-            pltpu.VMEM((LANES, 2 * LANES), BF16),
-            pltpu.VMEM((blocks, PIX, LANES), F32),
-            pltpu.VMEM((blocks, PIX, LANES), BF16),
-            pltpu.VMEM((blocks, PIX, LANES), BF16),
-            pltpu.VMEM((blocks, ROWS, LANES), F32),
+            pltpu.VMEM((BLOCK, BLOCK + LANES), BF16),
+            pltpu.VMEM((BLOCK, BLOCK + LANES), BF16),
+            pltpu.VMEM((blocks, PIX, BLOCK), F32),
+            pltpu.VMEM((blocks, PIX, BLOCK), BF16),
+            pltpu.VMEM((blocks, PIX, BLOCK), BF16),
+            pltpu.VMEM((blocks, ROWS, BLOCK), F32),
             pltpu.VMEM((PIX, LANES), F32),
             pltpu.VMEM((8, PIX), F32),
             pltpu.VMEM((slots // LANES * 32, LANES), F32),
@@ -704,7 +709,7 @@
         tile_ids,
         tile_counts,
         arrived,
-        tile_lists[0].reshape(tiles * blocks, LANES),
+        tile_lists[0].reshape(tiles * blocks, BLOCK),
         targets[0],
     )
     mine = lax.dynamic_slice_in_dim(wide, lax.axis_index("cam") * size, size, axis=1)

time: 61.5 us -> 52.7 us (0.86)
  Pallas kernels: 54.2 us -> 45.4 us
    pallas_call x1, Pallas kernels: 29 us -> 20.3 us  [per_device(): pl.pallas_call(functools.partial(render_kernel, tiles, blocks), out_shape...]
where the time goes in v1:
time: 52.7 us; the launch traced here: 52.5 us
  Pallas kernels  45.4 us (86%)
  local copies, waits for them, and re-layouts  5.64 us (11%)
  between operations  0.76 us (1%)
  other arithmetic  0.67 us (1%)
    pallas_call x1, Pallas kernels, per_device(): pl.pallas_call(functools.partial(render_kernel, tiles, blocks), out_shape...  20.3 us
    pallas_call x1, Pallas kernels, per_device(): pl.pallas_call(functools.partial(return_kernel, shards, cams, centre), ou...  12.7 us
    pallas_call x1, Pallas kernels, per_device(): pl.pallas_call(functools.partial(send_kernel, shards), out_shape=jax.Shap...  10 us
    unnamed x18, local copies, waits for them, and re-layouts  5.54 us
    pallas_call x1, Pallas kernels, per_device(): pl.pallas_call(functools.partial(project_kernel, centre), out_shape=(jax....  2.43 us

profile of v1, /device:TPU:0, one launch (start us, length us, event | category | flops | bytes accessed | tf_op | source)
XLA Modules:
  0.0 52.5 jit_solution(7610709091724825410)
XLA Ops:
  0.6 1.4 %copy.11 = f32[8,8,32,128]{3,2,1,0:T(8,128)S(1)} copy(f32[8,8,32,128]{3,1,2,0:T(8,128)} %bitcast.14) | data formatting | bytes 2097152
  2.0 0.0 copy-start
  2.1 0.1 slice.par_ref
  2.1 0.6 %copy-done = f32[2,4]{1,0:T(2,128)S(1)} copy-done((f32[2,4]{1,0:T(2,128)S(1)}, f32[2,4]{1,0:T(2,128)}, u32[]{:S(2)}) %copy-start) | copy-done | bytes 56
  2.7 0.0 copy-start.5
  2.7 2.4 %project.1 = (bf16[864,128]{1,0:T(8,128)(2,1)S(1)}, f32[3,32,128]{2,1,0:T(8,128)S(1)}) custom-call(f32[2,4]{1,0:T(2,128)S(1)} %copy-done, f32[59,32,128]{2,1,0:T(8,128)S(1)} %slice.par_ref), custom_call_target="tpu_custom_call" | custom-call | tf_op jit(solution)/shard_map/project/pallas_call | solution.py:659
  5.2 0.5 broadcast.3
  5.7 0.0 copy-done.5
  5.7 0.7 %reduce.3 = s32[2048]{0:T(1024)S(1)} reduce(s32[1,1,2048]{2,1,0:T(1,128)S(1)} %copy-done.5, s32[]{:T(128)} %broadcast.3), dimensions={0,1}, to_apply=%param.9.reduce_sub_computation.3 | reduce | bytes 16388 | tf_op args[2]
  6.4 0.0 copy-start.4
  6.4 10.0 %send.1.feats_ref = f32[8,16,256]{2,1,0:T(8,128)S(1)} custom-call(bf16[864,128]{1,0:T(8,128)(2,1)S(1)} %get-tuple-element.6.table, s32[8,256]{1,0:T(8,128)S(1)} %reshape.14.rows_ref), custom_call_target="tpu_custom_call" | custom-call | tf_op jit(solution)/shard_map/send/pallas_call | solution.py:671
  16.4 0.0 copy-done.4
  16.4 0.0 copy-start.3
  16.4 0.7 %copy-done.3 = f32[1,8,3,256]{3,1,2,0:T(8,128)S(1)} copy-done((f32[1,8,3,256]{3,1,2,0:T(8,128)S(1)}, f32[1,8,3,256]{3,1,2,0:T(8,128)}, u32[]{:S(2)}) %copy-start.3) | copy-done | bytes 24600
  17.2 0.0 copy-start.1
  17.2 0.0 copy-start.2
  17.2 0.6 %copy-done.1 = s32[1,8]{1,0:T(1,128)S(1)} copy-done((s32[1,8]{1,0:T(1,128)S(1)}, s32[1,8]{1,0:T(1,128)}, u32[]{:S(2)}) %copy-start.1) | copy-done | bytes 56
  17.8 0.0 copy-done.2
  17.8 20.3 %render.1 = (f32[8,3,256]{2,1,0:T(4,128)S(1)}, f32[8,16,256]{2,1,0:T(8,128)S(1)}) custom-call(s32[1,8]{1,0:T(1,128)S(1)} %copy-done.1, s32[1,8]{1,0:T(1,128)S(1)} %copy-done.2, f32[8,16,256]{2,1,0:T(8,128)S(1)} %send.1.feats_ref, s32[16,256]{1,0:T(8,128)S(1)} %reshape_squeeze.3.lists_ref, f32[8,3,256]{2,1,0:T(4,128)S(1)} %bitcast.10), custom_call_target="tpu_custom_call" | custom-call | tf_op jit(solution)/shard_map/render/pallas_call | solution.py:685
  38.1 0.6 %copy.10 = f32[1,8,3,256]{3,1,2,0:T(8,128)} copy(f32[1,8,3,256]{3,2,1,0:T(4,128)S(1)} %bitcast.11) | data formatting | bytes 49152
  38.8 12.7 %return_pull.1 = f32[59,16,128]{2,1,0:T(8,128)S(1)} custom-call(f32[2,4]{1,0:T(2,128)S(1)} %copy-done, f32[59,16,128]{2,1,0:T(8,128)S(1)} %constant_dynamic-slice_fusion.par_ref, f32[8,16,256]{2,1,0:T(8,128)S(1)} %get-tuple-element.8.slot_ref, s32[8,256]{1,0:T(8,128)S(1)} %reshape.14.rows_ref, f32[3,32,128]{2,1,0:T(8,128)S(1)} %get-tuple-element.9.gate_ref), custom_call_target="tpu_custom_call" | custom-call | tf_op jit(solution)/shard_map/return_pull/pallas_call | solution.py:716
  51.5 1.0 %copy.12 = f32[8,8,16,128]{3,1,2,0:T(8,128)} copy(f32[8,8,16,128]{3,2,1,0:T(8,128)S(1)} %bitcast.13) | data formatting | bytes 1048576
  (5 shorter events, 0.1 us)
Async XLA Ops:
  2.0 0.7 %copy-start = (f32[2,4]{1,0:T(2,128)S(1)}, f32[2,4]{1,0:T(2,128)}, u32[]{:S(2)}) copy-start(f32[2,4]{1,0:T(2,128)} %cam_ref.3) | copy-start | bytes 100
  2.7 3.0 %copy-start.5 = (s32[1,1,2048]{2,1,0:T(1,128)S(1)}, s32[1,1,2048]{2,1,0:T(1,128)}, u32[]{:S(2)}) copy-start(s32[1,1,2048]{2,1,0:T(1,128)} %param.9) | copy-start | bytes 24580
  6.4 10.0 %copy-start.4 = (s32[1,8,512]{2,1,0:T(8,128)S(1)}, s32[1,8,512]{2,1,0:T(8,128)}, u32[]{:S(2)}) copy-start(s32[1,8,512]{2,1,0:T(8,128)} %param.12) | copy-start | bytes 49156
  16.4 0.7 %copy-start.3 = (f32[1,8,3,256]{3,1,2,0:T(8,128)S(1)}, f32[1,8,3,256]{3,1,2,0:T(8,128)}, u32[]{:S(2)}) copy-start(f32[1,8,3,256]{3,1,2,0:T(8,128)} %param.13) | copy-start | bytes 73732
  17.2 0.7 %copy-start.1 = (s32[1,8]{1,0:T(1,128)S(1)}, s32[1,8]{1,0:T(1,128)}, u32[]{:S(2)}) copy-start(s32[1,8]{1,0:T(1,128)} %ids_ref.1) | copy-start | bytes 100
  17.2 0.7 %copy-start.2 = (s32[1,8]{1,0:T(1,128)S(1)}, s32[1,8]{1,0:T(1,128)}, u32[]{:S(2)}) copy-start(s32[1,8]{1,0:T(1,128)} %counts_ref.1) | copy-start | bytes 100
